TPU v7x, 32 devices: a whole 2x2x4 slice. The times are simulated.
32 devices in a mesh: lat: 4 (over x, core), lon: 8 (over z, y).
Axes of the slice: x: 2, y: 2, z: 4, core: 2. Of those that a mesh axis runs over, the one named last changes fastest.
Arguments:
- tokens: bfloat16 [4, 96, 96, 512], P(None, 'lat', 'lon'), may hold values from -6 to 6
- cotangent: bfloat16 [4, 96, 96, 512], P(None, 'lat', 'lon'), may hold values from -6 to 6
- w_qkv: bfloat16 [512, 1536], replicated, may hold values from -2 to 2
- w_proj: bfloat16 [512, 512], replicated, may hold values from -0.25 to 0.25
- shifts: int32 [4, 2], replicated, may hold values from 0 to 11, as said below
- region_ids: int32 [96], replicated, may hold values from 0 to 1999, as said below
Outputs:
- mixed: bfloat16 [4, 96, 96, 512], P(None, 'lat', 'lon')
- grad_tokens: bfloat16 [4, 96, 96, 512], P(None, 'lat', 'lon')
- grad_qkv: float32 [512, 1536], replicated
- grad_proj: float32 [512, 512], replicated
Inputs may be any that keep to these rules, and one draw needn't show every extreme that they name: For each level l, shifts[l, 0] is below 6 and shifts[l, 1] below 12; some level has shifts[l, 0] = 5 and some level has shifts[l, 1] = 11. region_ids is one positive label on the first 1 to 5 rows, another, larger positive label on the last 1 to 5 rows, and 0 on all others.
All inputs are finite; a program needn't handle non-finite values.
Results may differ from a plain program's by a relative error of at most 0.006.
The roundings to bfloat16 on the way count: a program that leaves them out, or rounds other values in their place, can miss the bound.
Values may be sent and summed in bfloat16 or wider, within the bound.
No kernel may reach another device: no remote copies, remote signals or barrier semaphores. Data moves between devices by JAX's collectives and lax.ppermute only.
A program may use at most 128 MiB of HBM per device.

v0:
```python
import math

import jax
import jax.numpy as jnp
from jax import lax
from jax.sharding import PartitionSpec as P

HEADS = 16
WLAT = 6
WLON = 12


NORM_EPS = 1e-05
FULL_PRECISION = lax.Precision.HIGHEST


def shifted(block, axis, distance):
    devices = range(lax.axis_size(axis))
    route = [((i - distance) % len(devices), i) for i in devices]
    return lax.ppermute(block, axis, route)


def slice_levels(grid_field, starts, length, axis):

    def per_level(level_plane, offset):
        return lax.dynamic_slice_in_dim(level_plane, offset, length, axis - 1)

    return jax.vmap(per_level)(grid_field, starts)


def make_windows(grid_field):
    lev_count, grid_rows, grid_cols, model_width = grid_field.shape
    shaped = grid_field.reshape(
        lev_count, grid_rows // WLAT, WLAT, grid_cols // WLON, WLON, model_width
    )
    shaped = shaped.transpose(1, 3, 0, 2, 4, 5)
    return shaped.reshape(-1, 2, lev_count * WLAT * WLON, model_width)


def undo_windows(blocks, lev_count, grid_rows, grid_cols):
    model_width = blocks.shape[-1]
    shaped = blocks.reshape(
        grid_rows // WLAT, grid_cols // WLON, lev_count, WLAT, WLON, model_width
    )
    return shaped.transpose(2, 0, 3, 1, 4, 5).reshape(lev_count, grid_rows, grid_cols, model_width)


def window_labels(rolled_ids, grid_cols):
    lev_count, grid_rows = rolled_ids.shape
    shaped = rolled_ids.reshape(lev_count, grid_rows // WLAT, WLAT)
    full = jnp.broadcast_to(
        shaped[:, :, :, None, None], (lev_count, grid_rows // WLAT, WLAT, grid_cols // WLON, WLON)
    )
    return full.transpose(1, 3, 0, 2, 4).reshape(-1, 2, lev_count * WLAT * WLON)


def window_forward(tile, labels, w_qkv, w_proj):
    tile_len, model_width = tile.shape
    head_size = model_width // HEADS
    values_full = tile.astype(jnp.float32)
    center = values_full - jnp.mean(values_full, axis=1, keepdims=True)
    variance = jnp.mean(center * center, axis=1, keepdims=True)
    inv_scale = lax.rsqrt(variance + NORM_EPS)
    standard = center * inv_scale
    normed = standard.astype(jnp.bfloat16)
    projected = jnp.dot(normed, w_qkv, preferred_element_type=jnp.float32)
    queries = projected[:, :model_width].reshape(tile_len, HEADS, head_size)
    key_rows = projected[:, model_width : 2 * model_width].reshape(tile_len, HEADS, head_size)
    value_rows = (
        projected[:, 2 * model_width :].astype(jnp.bfloat16).reshape(tile_len, HEADS, head_size)
    )
    scores = jnp.einsum("nhe,mhe->hnm", queries, key_rows, precision=FULL_PRECISION) / math.sqrt(
        head_size
    )
    allowed = labels[:, None] == labels[None, :]
    scores = jnp.where(allowed[None, :, :], scores, -jnp.inf)
    top_score = jnp.max(scores, axis=-1, keepdims=True)
    expo = jnp.exp(scores - top_score)
    weights = expo / jnp.sum(expo, axis=-1, keepdims=True)
    rounded_weights = weights.astype(jnp.bfloat16)
    context = jnp.einsum(
        "hnm,mhe->nhe", rounded_weights, value_rows, preferred_element_type=jnp.float32
    )
    context = context.reshape(tile_len, model_width).astype(jnp.bfloat16)
    update = jnp.dot(context, w_proj, preferred_element_type=jnp.float32).astype(jnp.bfloat16)
    stored = (
        standard,
        inv_scale,
        normed,
        queries,
        key_rows,
        value_rows,
        weights,
        rounded_weights,
        context,
    )
    return (update, stored)


def window_backward(stored, grad_tile, w_qkv, w_proj):
    (
        standard,
        inv_scale,
        normed,
        queries,
        key_rows,
        value_rows,
        weights,
        rounded_weights,
        context,
    ) = stored
    tile_len, model_width = grad_tile.shape
    head_size = model_width // HEADS
    grad_context = jnp.einsum(
        "nf,df->nd", grad_tile, w_proj, preferred_element_type=jnp.float32
    ).astype(jnp.bfloat16)
    grad_context = grad_context.reshape(tile_len, HEADS, head_size)
    proj_term = jnp.einsum("nd,nf->df", context, grad_tile, preferred_element_type=jnp.float32)
    grad_weights = jnp.einsum(
        "nhe,mhe->hnm", grad_context, value_rows, preferred_element_type=jnp.float32
    )
    grad_values = jnp.einsum(
        "hnm,nhe->mhe", rounded_weights, grad_context, preferred_element_type=jnp.float32
    )
    grad_scores = (
        weights
        * (grad_weights - jnp.sum(weights * grad_weights, axis=-1, keepdims=True))
        / math.sqrt(head_size)
    )
    grad_queries = jnp.einsum("hnm,mhe->nhe", grad_scores, key_rows, precision=FULL_PRECISION)
    grad_keys = jnp.einsum("hnm,nhe->mhe", grad_scores, queries, precision=FULL_PRECISION)
    grad_projected = jnp.concatenate(
        [
            grad_queries.reshape(tile_len, model_width),
            grad_keys.reshape(tile_len, model_width),
            grad_values.reshape(tile_len, model_width),
        ],
        axis=1,
    ).astype(jnp.bfloat16)
    qkv_term = jnp.einsum("nd,nf->df", normed, grad_projected, preferred_element_type=jnp.float32)
    grad_normed = jnp.einsum("nf,df->nd", grad_projected, w_qkv, preferred_element_type=jnp.float32)
    grad_input = inv_scale * (
        grad_normed
        - jnp.mean(grad_normed, axis=1, keepdims=True)
        - standard * jnp.mean(grad_normed * standard, axis=1, keepdims=True)
    )
    return (grad_input.astype(jnp.bfloat16), qkv_term, proj_term)


def run_groups(blocks, cot_blocks, labels, w_qkv, w_proj):
    model_width = blocks.shape[-1]

    def single(tile, grad_tile, label_row):
        update, stored = window_forward(tile, label_row, w_qkv, w_proj)
        grad_input, qkv_term, proj_term = window_backward(stored, grad_tile, w_qkv, w_proj)
        return (update, grad_input, qkv_term, proj_term)

    def group_step(totals, inputs):
        tile_set, grad_set, label_set = inputs
        update, grad_input, qkv_terms, proj_terms = jax.vmap(single)(tile_set, grad_set, label_set)
        return (
            (totals[0] + jnp.sum(qkv_terms, axis=0), totals[1] + jnp.sum(proj_terms, axis=0)),
            (update, grad_input),
        )

    zero_totals = (
        jnp.zeros((model_width, 3 * model_width), jnp.float32),
        jnp.zeros((model_width, model_width), jnp.float32),
    )
    return lax.scan(group_step, zero_totals, (blocks, cot_blocks, labels))


def join_ahead_cols(grid_field, ahead_block, lon_offsets):
    lon_cols = grid_field.shape[2]
    return slice_levels(
        jnp.concatenate([grid_field, ahead_block], axis=2), lon_offsets, lon_cols, 2
    )


def join_ahead_rows(grid_field, below_rows, lat_offsets):
    lat_rows = grid_field.shape[1]
    return slice_levels(jnp.concatenate([grid_field, below_rows], axis=1), lat_offsets, lat_rows, 1)


def join_behind_rows(grid_field, above_rows, lat_offsets):
    lat_rows = grid_field.shape[1]
    return slice_levels(
        jnp.concatenate([above_rows, grid_field], axis=1), WLAT - lat_offsets, lat_rows, 1
    )


def join_behind_cols(grid_field, left_block, lon_offsets):
    lon_cols = grid_field.shape[2]
    return slice_levels(
        jnp.concatenate([left_block, grid_field], axis=2), lon_cols - lon_offsets, lon_cols, 2
    )


def local(tokens, cotangent, w_qkv, w_proj, shifts, region_ids):
    lev_count, lat_rows, lon_cols, model_width = tokens.shape
    lat_offsets = shifts[:, 0]
    lon_offsets = shifts[:, 1]
    grid_rows = lat_rows * lax.axis_size("lat")
    first_row = lax.axis_index("lat") * lat_rows
    rows_wanted = (
        first_row + lat_offsets[:, None] + jnp.arange(lat_rows, dtype=jnp.int32)[None, :]
    ) % grid_rows
    table_rows = jnp.arange(grid_rows, dtype=jnp.int32)
    rolled_ids = jnp.sum(
        jnp.where(
            rows_wanted[:, :, None] == table_rows[None, None, :], region_ids[None, None, :], 0
        ),
        axis=2,
    )
    labels = window_labels(rolled_ids, lon_cols)
    ahead_tokens, ahead_cot = shifted((tokens, cotangent), "lon", -1)
    cols_tokens = join_ahead_cols(tokens, ahead_tokens, lon_offsets)
    cols_cot = join_ahead_cols(cotangent, ahead_cot, lon_offsets)
    below_tokens, below_cot = shifted((cols_tokens[:, :WLAT], cols_cot[:, :WLAT]), "lat", -1)
    rolled = join_ahead_rows(cols_tokens, below_tokens, lat_offsets)
    rolled_cot = join_ahead_rows(cols_cot, below_cot, lat_offsets)
    (qkv_total, proj_total), (updates, grads_back) = run_groups(
        make_windows(rolled), make_windows(rolled_cot), labels, w_qkv, w_proj
    )
    update_field = undo_windows(updates, lev_count, lat_rows, lon_cols)
    grad_field = undo_windows(grads_back, lev_count, lat_rows, lon_cols)
    above_update, above_grad = shifted(
        (update_field[:, lat_rows - WLAT :], grad_field[:, lat_rows - WLAT :]), "lat", 1
    )
    update_field = join_behind_rows(update_field, above_update, lat_offsets)
    grad_field = join_behind_rows(grad_field, above_grad, lat_offsets)
    left_update, left_grad = shifted((update_field, grad_field), "lon", 1)
    update_field = join_behind_cols(update_field, left_update, lon_offsets)
    grad_field = join_behind_cols(grad_field, left_grad, lon_offsets)
    mixed = (tokens.astype(jnp.float32) + update_field.astype(jnp.float32)).astype(jnp.bfloat16)
    grad_tokens = (cotangent.astype(jnp.float32) + grad_field.astype(jnp.float32)).astype(
        jnp.bfloat16
    )
    qkv_sum, proj_sum = lax.psum((qkv_total, proj_total), ("lat", "lon"))
    total_tokens = lev_count * grid_rows * lon_cols * lax.axis_size("lon")
    grad_scale = 1.0 / math.sqrt(total_tokens)
    return (mixed, grad_tokens, qkv_sum * grad_scale, proj_sum * grad_scale)


def solution(mesh):
    return jax.shard_map(
        local,
        mesh=mesh,
        in_specs=(P(None, "lat", "lon", None), P(None, "lat", "lon", None), P(), P(), P(), P()),
        out_specs=(P(None, "lat", "lon", None), P(None, "lat", "lon", None), P(), P()),
        check_vma=False,
    )
```

profile of v0, /device:TPU:0, one launch (start us, length us, event | category | flops | bytes accessed | tf_op | source)
XLA Modules:
  0.0 562.7 jit_solution(14866819949009429185)
XLA Ops:
  7.2 2.5 copy.123
  9.7 6.0 %collective-permute-start.2 = (bf16[4,24,12,512]{3,1,0,2:T(8,128)(2,1)}, bf16[4,24,12,512]{3,1,0,2:T(8,128)(2,1)}, u32[]{:S(2)}, u32[]{:S(2)}) collective-permute-start(bf16[4,24,12,512]{3,1,0,2:T(8,128)(2,1)} %copy.123), channel_id=1, source_target_pairs={{1,0},{2,1},{3,2},{4,3},{5,4},{6,5},{7,6},{0,7},{9,8},{10,9},{11,1... | collective-permute-start | bytes 3538952 | tf_op jit(solution)/shard_map/ppermute | solution.py:20
  18.4 24.0 %collective-permute-done.2 = bf16[4,24,12,512]{3,1,0,2:T(8,128)(2,1)} collective-permute-done((bf16[4,24,12,512]{3,1,0,2:T(8,128)(2,1)}, bf16[4,24,12,512]{3,1,0,2:T(8,128)(2,1)}, u32[]{:S(2)}, u32[]{:S(2)}) %collective-permute-start.2) | collective-permute-done | bytes 1179680 | tf_op jit(solution)/shard_map/ppermute | solution.py:20
  42.4 3.0 pad_maximum_fusion.4
  45.4 2.3 gather_fusion.2
  48.5 18.1 %collective-permute-done = bf16[4,24,12,512]{3,1,0,2:T(8,128)(2,1)} collective-permute-done((bf16[4,24,12,512]{3,1,0,2:T(8,128)(2,1)}, bf16[4,24,12,512]{3,1,0,2:T(8,128)(2,1)}, u32[]{:S(2)}, u32[]{:S(2)}) %collective-permute-start) | collective-permute-done | bytes 1179680 | tf_op jit(solution)/shard_map/ppermute | solution.py:20
  66.6 3.0 pad_maximum_fusion.3
  69.5 2.3 gather_fusion
  73.1 2.2 copy.124
  75.2 3.3 gather_fusion.3
  78.6 3.5 copy.173
  82.1 2.9 reshape.126
  86.1 1.8 gather_fusion.1
  87.9 3.5 copy.174
  91.4 3.8 reshape.123
  95.2 279.7 %while.17 = (s32[]{:T(128)}, f32[512,1536]{1,0:T(8,128)}, f32[512,512]{1,0:T(8,128)}, bf16[2,2,288,512]{3,1,0,2:T(2,128)(2,1)}, bf16[2,2,288,512]{3,1,0,2:T(2,12...) while((s32[]{:T(128)}, f32[512,1536]{1,0:T(8,128)}, ...), condition=%wide.region_9.10_spmd.clone, body=%wide.region_1.9_spmd.clone.sunk | while | flops 7269771264 | bytes 272412032 | solution.py:170
  119.5 1.5 constant_dynamic-slice_fusion.5
  128.2 1.7 copy.199
  129.9 1.7 copy.200
  131.6 15.7 %fusion.130 = f32[2,16,288,288]{2,3,1,0:T(8,128)} fusion(f32[2,288,16,32]{1,3,2,0:T(8,128)S(1)} %bitcast.184, f32[2,288,16,32]{1,3,2,0:T(8,128)} %bitcast.186), kind=kOutput, calls=%fused_computation.119.clone.1 | convolution fusion | flops 1019215872 | bytes 12976128 | tf_op jit(solution)/shard_map/while/body/eval_jaxpr/vmap(nhe,mhe->hnm)/dot_general | solution.py:72
  147.3 17.2 %fusion.131 = (f32[2,16,288]{2,1,0:T(8,128)S(1)}, f32[2,16,288,288]{2,3,1,0:T(8,128)}) fusion(f32[2,16,288,288]{2,3,1,0:T(8,128)} %fusion.130, pred[2,288,288]{1,2,0:T(8,128)(4,1)S(1)} %copy-done.22), kind=kOutput, calls=%fused_computation.118.clone.1 | output fusion | flops 15925535 | bytes 21436416 | tf_op jit(solution)/shard_map/while/body/eval_jaxpr/vmap()/sub | solution.py:78
  164.6 6.4 %fusion.136 = bf16[2,16,32,288]{3,2,1,0:T(8,128)(2,1)S(1)} fusion(bf16[2,288,16,32]{1,3,2,0:T(8,128)(2,1)S(1)} %bitcast.191, f32[2,16,288,288]{2,3,1,0:T(8,128)} %get-tuple-element.240, f32[2,16,288]{2,1,0:T(8,128)S(1)} %get-tuple-element.241), kind=kOutput, calls=%fused_computation.34.clone.1 | convolution fusion | flops 175472640 | bytes 11833344 | tf_op jit(solution)/shard_map/while/body/eval_jaxpr/vmap(hnm,mhe->nhe)/dot_general | solution.py:81
  173.7 8.0 %fusion.132 = bf16[2,16,32,288]{3,2,1,0:T(8,128)(2,1)} fusion(bf16[2,288,16,32]{1,3,2,0:T(8,128)(2,1)S(1)} %bitcast.189, f32[2,16,288,288]{2,3,1,0:T(8,128)} %get-tuple-element.240, f32[2,16,288]{2,1,0:T(8,128)S(1)} %get-tuple-element.241), kind=kOutput, calls=%fused_computation.33.clone.1 | convolution fusion | flops 175472640 | bytes 11833344 | tf_op jit(solution)/shard_map/while/body/eval_jaxpr/vmap(hnm,nhe->mhe)/dot_general | solution.py:122
  181.7 1.4 copy.201
  183.1 12.8 %multiply_reduce_fusion.2 = (f32[2,16,288]{2,1,0:T(8,128)S(1)}, f32[2,16,288,288]{2,3,1,0:T(8,128)}) fusion(f32[2,16,288,288]{2,3,1,0:T(8,128)} %get-tuple-element.240, f32[2,16,288]{2,1,0:T(8,128)} %copy-done.36, bf16[2,288,16,32]{1,3,2,0:T(8,128)(2,1)} %bitcast.188, bf16[2,288,16,32]{1,3,2,0:T(8,128)(2,1)} %bitcast.190), kind=kOutput, calls=%fused_computation.10.clone.1 | convolution fusion | flops 177822720 | bytes 22487040 | tf_op jit(solution)/shard_map/while/body/eval_jaxpr/vmap(nhe,mhe->hnm)/dot_general | solution.py:119
  195.9 15.3 %fusion.134 = bf16[2,16,32,288]{3,2,1,0:T(8,128)(2,1)S(1)} fusion(f32[2,288,16,32]{1,3,2,0:T(8,128)S(1)} %bitcast.187, f32[2,16,288,288]{2,3,1,0:T(8,128)} %get-tuple-element.242, f32[2,16,288]{2,1,0:T(8,128)S(1)} %get-tuple-element.243, f32[2,16,288,288]{2,3,1,0:T(8,128)} %get-tuple-element.240, f32[2,16,288]{2,1,0:T(8,128)S(1)} %copy-done.37), kind=kOutput, calls=%fused_computation.35.clone.1 | convolution fusion | flops 1030127616 | bytes 23076864 | tf_op jit(solution)/shard_map/while/body/eval_jaxpr/vmap(hnm,mhe->nhe)/dot_general | solution.py:130
  211.1 19.2 %fusion.133 = bf16[2,16,32,288]{3,2,1,0:T(8,128)(2,1)} fusion(f32[2,288,16,32]{1,3,2,0:T(8,128)S(1)} %bitcast.185, f32[2,16,288,288]{2,3,1,0:T(8,128)} %get-tuple-element.242, f32[2,16,288]{2,1,0:T(8,128)S(1)} %get-tuple-element.243, f32[2,16,288,288]{2,3,1,0:T(8,128)} %get-tuple-element.240, f32[2,16,288]{2,1,0:T(8,128)S(1)} %copy-done.37), kind=kOutput, calls=%fused_computation.36.clone.1 | convolution fusion | flops 1030127616 | bytes 23076864 | tf_op jit(solution)/shard_map/while/body/eval_jaxpr/vmap(hnm,nhe->mhe)/dot_general | solution.py:131
  230.3 2.4 copy.203
  233.8 2.6 fusion.138
  237.7 2.0 fusion.135
  239.8 1.4 copy_dynamic-update-slice_fusion.3
  243.7 1.5 constant_dynamic-slice_fusion.5
  252.4 1.7 copy.199
  254.1 1.7 copy.200
  255.8 15.7 %fusion.130 = f32[2,16,288,288]{2,3,1,0:T(8,128)} fusion(f32[2,288,16,32]{1,3,2,0:T(8,128)S(1)} %bitcast.184, f32[2,288,16,32]{1,3,2,0:T(8,128)} %bitcast.186), kind=kOutput, calls=%fused_computation.119.clone.1 | convolution fusion | flops 1019215872 | bytes 12976128 | tf_op jit(solution)/shard_map/while/body/eval_jaxpr/vmap(nhe,mhe->hnm)/dot_general | solution.py:72
  271.5 17.2 %fusion.131 = (f32[2,16,288]{2,1,0:T(8,128)S(1)}, f32[2,16,288,288]{2,3,1,0:T(8,128)}) fusion(f32[2,16,288,288]{2,3,1,0:T(8,128)} %fusion.130, pred[2,288,288]{1,2,0:T(8,128)(4,1)S(1)} %copy-done.22), kind=kOutput, calls=%fused_computation.118.clone.1 | output fusion | flops 15925535 | bytes 21436416 | tf_op jit(solution)/shard_map/while/body/eval_jaxpr/vmap()/sub | solution.py:78
  288.8 6.4 %fusion.136 = bf16[2,16,32,288]{3,2,1,0:T(8,128)(2,1)S(1)} fusion(bf16[2,288,16,32]{1,3,2,0:T(8,128)(2,1)S(1)} %bitcast.191, f32[2,16,288,288]{2,3,1,0:T(8,128)} %get-tuple-element.240, f32[2,16,288]{2,1,0:T(8,128)S(1)} %get-tuple-element.241), kind=kOutput, calls=%fused_computation.34.clone.1 | convolution fusion | flops 175472640 | bytes 11833344 | tf_op jit(solution)/shard_map/while/body/eval_jaxpr/vmap(hnm,mhe->nhe)/dot_general | solution.py:81
  297.9 8.0 %fusion.132 = bf16[2,16,32,288]{3,2,1,0:T(8,128)(2,1)} fusion(bf16[2,288,16,32]{1,3,2,0:T(8,128)(2,1)S(1)} %bitcast.189, f32[2,16,288,288]{2,3,1,0:T(8,128)} %get-tuple-element.240, f32[2,16,288]{2,1,0:T(8,128)S(1)} %get-tuple-element.241), kind=kOutput, calls=%fused_computation.33.clone.1 | convolution fusion | flops 175472640 | bytes 11833344 | tf_op jit(solution)/shard_map/while/body/eval_jaxpr/vmap(hnm,nhe->mhe)/dot_general | solution.py:122
  305.9 1.4 copy.201
  307.3 12.8 %multiply_reduce_fusion.2 = (f32[2,16,288]{2,1,0:T(8,128)S(1)}, f32[2,16,288,288]{2,3,1,0:T(8,128)}) fusion(f32[2,16,288,288]{2,3,1,0:T(8,128)} %get-tuple-element.240, f32[2,16,288]{2,1,0:T(8,128)} %copy-done.36, bf16[2,288,16,32]{1,3,2,0:T(8,128)(2,1)} %bitcast.188, bf16[2,288,16,32]{1,3,2,0:T(8,128)(2,1)} %bitcast.190), kind=kOutput, calls=%fused_computation.10.clone.1 | convolution fusion | flops 177822720 | bytes 22487040 | tf_op jit(solution)/shard_map/while/body/eval_jaxpr/vmap(nhe,mhe->hnm)/dot_general | solution.py:119
  320.1 15.3 %fusion.134 = bf16[2,16,32,288]{3,2,1,0:T(8,128)(2,1)S(1)} fusion(f32[2,288,16,32]{1,3,2,0:T(8,128)S(1)} %bitcast.187, f32[2,16,288,288]{2,3,1,0:T(8,128)} %get-tuple-element.242, f32[2,16,288]{2,1,0:T(8,128)S(1)} %get-tuple-element.243, f32[2,16,288,288]{2,3,1,0:T(8,128)} %get-tuple-element.240, f32[2,16,288]{2,1,0:T(8,128)S(1)} %copy-done.37), kind=kOutput, calls=%fused_computation.35.clone.1 | convolution fusion | flops 1030127616 | bytes 23076864 | tf_op jit(solution)/shard_map/while/body/eval_jaxpr/vmap(hnm,mhe->nhe)/dot_general | solution.py:130
  335.3 19.2 %fusion.133 = bf16[2,16,32,288]{3,2,1,0:T(8,128)(2,1)} fusion(f32[2,288,16,32]{1,3,2,0:T(8,128)S(1)} %bitcast.185, f32[2,16,288,288]{2,3,1,0:T(8,128)} %get-tuple-element.242, f32[2,16,288]{2,1,0:T(8,128)S(1)} %get-tuple-element.243, f32[2,16,288,288]{2,3,1,0:T(8,128)} %get-tuple-element.240, f32[2,16,288]{2,1,0:T(8,128)S(1)} %copy-done.37), kind=kOutput, calls=%fused_computation.36.clone.1 | convolution fusion | flops 1030127616 | bytes 23076864 | tf_op jit(solution)/shard_map/while/body/eval_jaxpr/vmap(hnm,nhe->mhe)/dot_general | solution.py:131
  354.5 2.4 copy.203
  358.0 2.6 fusion.138
  361.9 2.1 fusion.135
  364.0 1.4 copy_dynamic-update-slice_fusion.3
  375.0 3.2 reshape.127
  379.8 3.2 reshape.129
  384.5 2.3 collective-permute-done.4
  386.9 3.0 pad_maximum_fusion.7
  389.9 2.4 gather_fusion.4
  392.3 1.7 copy.130
  394.1 2.6 pad_maximum_fusion.8
  396.7 3.4 gather_fusion.6
  400.1 2.1 copy.135
  402.8 39.6 %collective-permute-done.5 = bf16[4,24,12,512]{3,1,2,0:T(8,128)(2,1)S(1)} collective-permute-done((bf16[4,24,12,512]{3,1,2,0:T(8,128)(2,1)}, bf16[4,24,12,512]{3,1,2,0:T(8,128)(2,1)S(1)}, u32[]{:S(2)}, u32[]{:S(2)}) %collective-permute-start.5) | collective-permute-done | bytes 1179680 | tf_op jit(solution)/shard_map/ppermute | solution.py:20
  443.7 2.2 copy.132
  445.9 25.8 %collective-permute-done.7 = bf16[4,24,12,512]{3,1,2,0:T(8,128)(2,1)S(1)} collective-permute-done((bf16[4,24,12,512]{3,1,2,0:T(8,128)(2,1)S(1)}, bf16[4,24,12,512]{3,1,2,0:T(8,128)(2,1)S(1)}, u32[]{:S(2)}, u32[]{:S(2)}) %collective-permute-start.7) | collective-permute-done | bytes 1179680 | tf_op jit(solution)/shard_map/ppermute | solution.py:20
  472.9 2.2 copy.137
  475.1 3.3 gather_fusion.5
  478.5 3.5 gather_fusion.7
  481.9 3.7 add_convert_fusion
  485.6 65.0 %all-reduce.5.cloned.1.call-done = (f32[512,1536]{1,0:T(8,128)}, f32[512,512]{1,0:T(8,128)}) async-done(((f32[512,1536]{1,0:T(8,128)}, f32[512,512]{1,0:T(8,128)}), (f32[512,1536]{1,0:T(8,128)}, f32[512,512]{1,0:T(8,128)})) %all-reduce.5.cloned.1.call-update) | async-done | bytes 4194320 | tf_op jit(solution)/shard_map/psum | solution.py:239
  550.6 4.0 broadcast_multiply_fusion.3
  (200 shorter events, 42.6 us)
Async XLA Ops:
  7.2 8.6 %copy-start.15 = (bf16[4,24,12,512]{3,1,2,0:T(8,128)(2,1)S(1)}, bf16[4,24,12,512]{3,1,2,0:T(8,128)(2,1)}, u32[]{:S(2)}) copy-start(bf16[4,24,12,512]{3,1,2,0:T(8,128)(2,1)} %param.8) | copy-start | bytes 3538948
  7.2 543.5 %all-reduce.5.cloned.1.call-start = ((), (), s32[]{:S(2)}) async-start(), calls=%async_computation | async-start | bytes 8388608 | tf_op jit(solution)/shard_map/psum | solution.py:239
  9.7 7.7 %copy-start.32 = (s32[4,2]{0,1:T(2,128)S(1)}, s32[4,2]{0,1:T(2,128)}, u32[]{:S(2)}) copy-start(s32[4,2]{0,1:T(2,128)} %param.12) | copy-start | bytes 100
  9.7 8.4 %copy-start.33 = (s32[96]{0:T(128)S(1)}, s32[96]{0:T(128)}, u32[]{:S(2)}) copy-start(s32[96]{0:T(128)} %param.13) | copy-start | bytes 1156
  9.7 32.7 %copy-start.17 = (bf16[4,24,12,512]{3,1,2,0:T(8,128)(2,1)S(1)}, bf16[4,24,12,512]{3,1,2,0:T(8,128)(2,1)}, u32[]{:S(2)}) copy-start(bf16[4,24,12,512]{3,1,2,0:T(8,128)(2,1)} %param.9) | copy-start | bytes 3538948
  9.7 32.7 %collective-permute-start.2 = (bf16[4,24,12,512]{3,1,0,2:T(8,128)(2,1)}, bf16[4,24,12,512]{3,1,0,2:T(8,128)(2,1)}, u32[]{:S(2)}, u32[]{:S(2)}) collective-permute-start(bf16[4,24,12,512]{3,1,0,2:T(8,128)(2,1)} %copy.123), channel_id=1, source_target_pairs={{1,0},{2,1},{3,2},{4,3},{5,4},{6,5},{7,6},{0,7},{9,8},{10,9},{11,1... | collective-permute-start | bytes 3538952 | tf_op jit(solution)/shard_map/ppermute | solution.py:20
  16.9 49.7 %collective-permute-start = (bf16[4,24,12,512]{3,1,0,2:T(8,128)(2,1)}, bf16[4,24,12,512]{3,1,0,2:T(8,128)(2,1)}, u32[]{:S(2)}, u32[]{:S(2)}) collective-permute-start(bf16[4,24,12,512]{3,1,0,2:T(8,128)(2,1)} %copy.118), channel_id=1, source_target_pairs={{1,0},{2,1},{3,2},{4,3},{5,4},{6,5},{7,6},{0,7},{9,8},{10,9},{11,1... | collective-permute-start | bytes 3538952 | tf_op jit(solution)/shard_map/ppermute | solution.py:20
  48.5 24.4 %collective-permute-start.3 = (bf16[4,6,12,512]{3,1,2,0:T(8,128)(2,1)}, bf16[4,6,12,512]{3,1,2,0:T(8,128)(2,1)S(1)}, u32[]{:S(2)}, u32[]{:S(2)}) collective-permute-start(bf16[4,6,12,512]{3,1,2,0:T(8,128)(2,1)} %slice.85), channel_id=1, source_target_pairs={{8,0},{16,8},{24,16},{0,24},{9,1},{17,9},{25,17},{1,25},{10,2},{18... | collective-permute-start | bytes 884744 | tf_op jit(solution)/shard_map/ppermute | solution.py:20
  72.6 12.4 %collective-permute-start.1 = (bf16[4,6,12,512]{3,1,2,0:T(8,128)(2,1)}, bf16[4,6,12,512]{3,1,2,0:T(8,128)(2,1)S(1)}, u32[]{:S(2)}, u32[]{:S(2)}) collective-permute-start(bf16[4,6,12,512]{3,1,2,0:T(8,128)(2,1)} %slice.84), channel_id=1, source_target_pairs={{8,0},{16,8},{24,16},{0,24},{9,1},{17,9},{25,17},{1,25},{10,2},{18... | collective-permute-start | bytes 884744 | tf_op jit(solution)/shard_map/ppermute | solution.py:20
  91.4 3.8 copy-start.3
  118.4 3.2 copy-start.12
  119.5 3.4 copy-start.34
  131.6 15.7 %copy-start.22 = (pred[2,288,288]{1,2,0:T(8,128)(4,1)S(1)}, pred[2,288,288]{1,2,0:T(8,128)(4,1)}, u32[]{:S(2)}) copy-start(pred[2,288,288]{1,2,0:T(8,128)(4,1)} %broadcast_compare_fusion.2) | copy-start | bytes 497668 | tf_op jit(solution)/shard_map/while
  147.3 17.2 %copy-start.8 = (bf16[2,288,512]{1,2,0:T(8,128)(2,1)S(1)}, bf16[2,288,512]{1,2,0:T(8,128)(2,1)}, u32[]{:S(2)}) copy-start(bf16[2,288,512]{1,2,0:T(8,128)(2,1)} %copy.202) | copy-start | bytes 1769476 | tf_op jit(solution)/shard_map/while
  164.5 8.9 %copy-start.36 = (f32[2,16,288]{2,1,0:T(8,128)}, f32[2,16,288]{2,1,0:T(8,128)S(1)}, u32[]{:S(2)}) copy-start(f32[2,16,288]{2,1,0:T(8,128)S(1)} %get-tuple-element.241) | copy-start | bytes 110596 | tf_op jit(solution)/shard_map/while
  164.5 6.4 %copy-start.2 = (bf16[1,2,288,512]{3,1,0,2:T(2,128)(2,1)S(1)}, bf16[1,2,288,512]{3,1,0,2:T(2,128)(2,1)}, u32[]{:S(2)}) copy-start(bf16[1,2,288,512]{3,1,0,2:T(2,128)(2,1)} %copy-done.1) | copy-start | bytes 1769476 | tf_op jit(solution)/shard_map/while
  164.6 6.4 %copy-start.5 = (f32[512,512]{1,0:T(8,128)S(1)}, f32[512,512]{1,0:T(8,128)}, u32[]{:S(2)}) copy-start(f32[512,512]{1,0:T(8,128)} %get-tuple-element.263) | copy-start | bytes 3145732 | tf_op jit(solution)/shard_map/while
  172.0 9.6 %copy-start.6 = (f32[512,512]{1,0:T(8,128)}, f32[512,512]{1,0:T(8,128)S(1)}, u32[]{:S(2)}) copy-start(f32[512,512]{1,0:T(8,128)S(1)} %fusion.137) | copy-start | bytes 3145732 | tf_op jit(solution)/shard_map/while
  172.0 1.7 copy-start.7
  183.1 12.8 %copy-start = (f32[2,288,512]{1,2,0:T(8,128)S(1)}, f32[2,288,512]{1,2,0:T(8,128)}, u32[]{:S(2)}) copy-start(f32[2,288,512]{1,2,0:T(8,128)} %copy.200) | copy-start | bytes 3538948 | tf_op jit(solution)/shard_map/while
  183.1 12.8 %copy-start.37 = (f32[2,16,288]{2,1,0:T(8,128)S(1)}, f32[2,16,288]{2,1,0:T(8,128)}, u32[]{:S(2)}) copy-start(f32[2,16,288]{2,1,0:T(8,128)} %copy-done.36) | copy-start | bytes 110596 | tf_op jit(solution)/shard_map/while
  230.3 3.5 copy-start.4
  233.8 3.1 copy-start.23
  236.5 1.2 copy-start.11
  237.7 2.1 copy-start.9
  237.7 2.1 copy-start.25
  237.7 2.1 copy-start.27
  239.8 1.7 copy-start.24
  239.8 2.8 copy-start.13
  241.3 1.4 copy-start.28
  242.6 3.1 copy-start.12
  243.7 3.4 copy-start.34
  255.8 15.7 %copy-start.22 = (pred[2,288,288]{1,2,0:T(8,128)(4,1)S(1)}, pred[2,288,288]{1,2,0:T(8,128)(4,1)}, u32[]{:S(2)}) copy-start(pred[2,288,288]{1,2,0:T(8,128)(4,1)} %broadcast_compare_fusion.2) | copy-start | bytes 497668 | tf_op jit(solution)/shard_map/while
  271.5 17.2 %copy-start.8 = (bf16[2,288,512]{1,2,0:T(8,128)(2,1)S(1)}, bf16[2,288,512]{1,2,0:T(8,128)(2,1)}, u32[]{:S(2)}) copy-start(bf16[2,288,512]{1,2,0:T(8,128)(2,1)} %copy.202) | copy-start | bytes 1769476 | tf_op jit(solution)/shard_map/while
  288.7 8.9 %copy-start.36 = (f32[2,16,288]{2,1,0:T(8,128)}, f32[2,16,288]{2,1,0:T(8,128)S(1)}, u32[]{:S(2)}) copy-start(f32[2,16,288]{2,1,0:T(8,128)S(1)} %get-tuple-element.241) | copy-start | bytes 110596 | tf_op jit(solution)/shard_map/while
  288.7 6.4 %copy-start.2 = (bf16[1,2,288,512]{3,1,0,2:T(2,128)(2,1)S(1)}, bf16[1,2,288,512]{3,1,0,2:T(2,128)(2,1)}, u32[]{:S(2)}) copy-start(bf16[1,2,288,512]{3,1,0,2:T(2,128)(2,1)} %copy-done.1) | copy-start | bytes 1769476 | tf_op jit(solution)/shard_map/while
  288.7 6.4 %copy-start.5 = (f32[512,512]{1,0:T(8,128)S(1)}, f32[512,512]{1,0:T(8,128)}, u32[]{:S(2)}) copy-start(f32[512,512]{1,0:T(8,128)} %get-tuple-element.263) | copy-start | bytes 3145732 | tf_op jit(solution)/shard_map/while
  296.2 9.6 %copy-start.6 = (f32[512,512]{1,0:T(8,128)}, f32[512,512]{1,0:T(8,128)S(1)}, u32[]{:S(2)}) copy-start(f32[512,512]{1,0:T(8,128)S(1)} %fusion.137) | copy-start | bytes 3145732 | tf_op jit(solution)/shard_map/while
  296.2 1.7 copy-start.7
  307.3 12.8 %copy-start = (f32[2,288,512]{1,2,0:T(8,128)S(1)}, f32[2,288,512]{1,2,0:T(8,128)}, u32[]{:S(2)}) copy-start(f32[2,288,512]{1,2,0:T(8,128)} %copy.200) | copy-start | bytes 3538948 | tf_op jit(solution)/shard_map/while
  307.3 12.8 %copy-start.37 = (f32[2,16,288]{2,1,0:T(8,128)S(1)}, f32[2,16,288]{2,1,0:T(8,128)}, u32[]{:S(2)}) copy-start(f32[2,16,288]{2,1,0:T(8,128)} %copy-done.36) | copy-start | bytes 110596 | tf_op jit(solution)/shard_map/while
  354.5 3.5 copy-start.4
  358.0 3.1 copy-start.23
  360.6 1.1 copy-start.10
  360.6 1.2 copy-start.11
  361.9 2.1 copy-start.9
  361.9 2.1 copy-start.25
  361.9 2.1 copy-start.27
  364.0 1.7 copy-start.24
  364.0 2.8 copy-start.13
  365.4 1.4 copy-start.28
  378.5 4.5 copy-start.21
  379.3 7.5 %collective-permute-start.4 = (bf16[4,6,12,512]{3,2,0,1:T(8,128)(2,1)}, bf16[4,6,12,512]{3,2,0,1:T(8,128)(2,1)}, u32[]{:S(2)}, u32[]{:S(2)}) collective-permute-start(bf16[4,6,12,512]{3,2,0,1:T(8,128)(2,1)} %slice.86), channel_id=1, source_target_pairs={{24,0},{0,8},{8,16},{16,24},{25,1},{1,9},{9,17},{17,25},{26,2},{2,... | collective-permute-start | bytes 884744 | tf_op jit(solution)/shard_map/ppermute | solution.py:20
  383.3 1.2 copy-start.19
  383.4 10.8 %collective-permute-start.6 = (bf16[4,6,12,512]{3,2,0,1:T(8,128)(2,1)S(1)}, bf16[4,6,12,512]{3,2,0,1:T(8,128)(2,1)}, u32[]{:S(2)}, u32[]{:S(2)}) collective-permute-start(bf16[4,6,12,512]{3,2,0,1:T(8,128)(2,1)S(1)} %slice.87), channel_id=1, source_target_pairs={{24,0},{0,8},{8,16},{16,24},{25,1},{1,9},{9,17},{17,25},{26,2},{2,... | collective-permute-start | bytes 884744 | tf_op jit(solution)/shard_map/ppermute | solution.py:20
  384.5 5.4 copy-start.31
  392.2 1.9 copy-start.20
  393.9 48.5 %collective-permute-start.5 = (bf16[4,24,12,512]{3,1,2,0:T(8,128)(2,1)}, bf16[4,24,12,512]{3,1,2,0:T(8,128)(2,1)S(1)}, u32[]{:S(2)}, u32[]{:S(2)}) collective-permute-start(bf16[4,24,12,512]{3,1,2,0:T(8,128)(2,1)} %copy.130), channel_id=1, source_target_pairs={{7,0},{0,1},{1,2},{2,3},{3,4},{4,5},{5,6},{6,7},{15,8},{8,9},{9,10... | collective-permute-start | bytes 3538952 | tf_op jit(solution)/shard_map/ppermute | solution.py:20
  402.2 69.5 %collective-permute-start.7 = (bf16[4,24,12,512]{3,1,2,0:T(8,128)(2,1)S(1)}, bf16[4,24,12,512]{3,1,2,0:T(8,128)(2,1)S(1)}, u32[]{:S(2)}, u32[]{:S(2)}) collective-permute-start(bf16[4,24,12,512]{3,1,2,0:T(8,128)(2,1)S(1)} %copy.135), channel_id=1, source_target_pairs={{7,0},{0,1},{1,2},{2,3},{3,4},{4,5},{5,6},{6,7},{15,8},{8,9},{9,10... | collective-permute-start | bytes 3538952 | tf_op jit(solution)/shard_map/ppermute | solution.py:20
  445.9 26.2 %copy-start.14 = (bf16[4,24,12,512]{3,2,1,0:T(8,128)(2,1)S(1)}, bf16[4,24,12,512]{3,2,1,0:T(8,128)(2,1)}, u32[]{:S(2)}) copy-start(bf16[4,24,12,512]{3,2,1,0:T(8,128)(2,1)} %gather_fusion.6) | copy-start | bytes 3538948
  472.9 2.2 copy-start.30
  478.5 3.5 copy-start.16
  478.5 3.5 copy-start.18
  550.6 4.0 copy-start.29
  (7 other events, 6.9 us)
Sparse Core Ops, SparseCore 0:
  384.6 165.9 all-reduce.4
where the time goes:
time: 570 us; the launch traced here: 563 us
  waiting for transfers between devices  175 us (31%)
  matrix products  171 us (30%)
  local copies, waits for them, and re-layouts  99.6 us (17%)
  other arithmetic  61.6 us (11%)
  loops' own time  31.9 us (6%)
  between operations  14.5 us (3%)
  starting transfers between devices  9.06 us (2%)
    ppermute x8, waiting for transfers between devices, shifted(): return lax.ppermute(block, axis, route)  110 us
    psum x1, waiting for transfers between devices, local(): qkv_sum, proj_sum = lax.psum((qkv_total, proj_total), ('lat', 'lon'))  65 us
    dot_general x2, matrix products, window_backward(): jnp.einsum('hnm,nhe->mhe', grad_scores, queries, precision=FULL_PRECISION)  38.4 us
    sub x2, other arithmetic, window_forward(): expo = jnp.exp(scores - top_score)  34.4 us
    another operation x1, loops' own time, run_groups(): return lax.scan(group_step, zero_totals, (blocks, cot_blocks, labels))  31.9 us
    dot_general x2, matrix products, window_forward(): jnp.einsum('nhe,mhe->hnm', queries, key_rows, precision=FULL_PRECISION)  31.4 us
    dot_general x2, matrix products, window_backward(): jnp.einsum('hnm,mhe->nhe', grad_scores, key_rows, precision=FULL_PRECISION)  30.5 us
    gather x10, local copies, waits for them, and re-layouts, per_level(): return lax.dynamic_slice_in_dim(level_plane, offset, length, axis - 1)  26 us
  transfers between devices with their start and end apart: 9, of which 6 were waited for; matrix products, arithmetic and copies ran while one was open for 11% of the time, Pallas kernels for 0%

commit v1 on v0

v1 whole, which is shorter than its diff:
```python
import functools
import math

import jax
import jax.numpy as jnp
from jax import lax
from jax.experimental import pallas as pl
from jax.experimental.pallas import tpu as pltpu
from jax.sharding import PartitionSpec as P

HEADS = 16
WLAT = 6
WLON = 12
NORM_EPS = 1e-05
LANES = 384
BARRED = 2.0**100
BF = jnp.bfloat16
F32 = jnp.float32

NN = (((1,), (0,)), ((), ()))
NT = (((1,), (1,)), ((), ()))
TN = (((0,), (0,)), ((), ()))


def dot(a, b, dims):
    return lax.dot_general(a, b, dims, preferred_element_type=F32)


def split_bf16(value):
    high = value.astype(BF)
    low = (value - high.astype(F32)).astype(BF)
    return high, low


def standardize(tile):
    values_full = tile.astype(F32)
    center = values_full - jnp.mean(values_full, axis=1, keepdims=True)
    variance = jnp.mean(center * center, axis=1, keepdims=True)
    inv_scale = lax.rsqrt(variance + NORM_EPS)
    return center * inv_scale, inv_scale


def window_kernel(
    x_ref, cot_ref, bar_q_ref, bar_k_ref, w_ref, wp_ref,
    update_ref, grad_ref, qkv_ref, proj_ref,
    norm_s, cot_s, q_s, k_s, v_s, g_s, ctx_s, gp_s,
):
    count, width = x_ref.shape
    size = width // HEADS

    @pl.when(pl.program_id(0) == 0)
    def _():
        qkv_ref[...] = jnp.zeros_like(qkv_ref)
        proj_ref[...] = jnp.zeros_like(proj_ref)
        norm_s[...] = jnp.zeros_like(norm_s)
        cot_s[...] = jnp.zeros_like(cot_s)

    standard, _ = standardize(x_ref[...])
    norm_s[:count] = standard.astype(BF)
    cot_s[:count] = cot_ref[...]
    scale = 1.0 / math.sqrt(size)
    q_s[...] = dot(w_ref[:width], norm_s[...], NT)
    k_s[...] = dot(w_ref[width : 2 * width], norm_s[...], NT)
    v_s[...] = dot(w_ref[2 * width :], norm_s[...], NT).astype(BF)
    g_s[...] = dot(wp_ref[...], cot_s[...], NT).astype(BF)

    def head(h, carry):
        rows = pl.ds(pl.multiple_of(h * size, size), size)
        q_high, q_low = split_bf16(q_s[rows] * (scale * math.log2(math.e)))
        k_high, k_low = split_bf16(k_s[rows])
        value = v_s[rows]
        grad_ctx = g_s[rows]
        q_all = jnp.concatenate([q_high, q_low, q_high, bar_q_ref[...]], axis=0)
        k_all = jnp.concatenate([k_high, k_high, k_low, bar_k_ref[...]], axis=0)
        k_tok = k_all.T[:count]
        v_tok = value.T[:count]
        scores = dot(k_tok, q_all, NN)
        expo = jnp.exp2(scores - jnp.max(scores, axis=0, keepdims=True))
        weights = expo * (1.0 / jnp.sum(expo, axis=0, keepdims=True))
        rounded = weights.astype(BF)
        ctx_s[rows] = dot(value[:, :count], rounded, NN)[:, :count].astype(BF)
        grad_w = dot(v_tok, grad_ctx, NN)
        grad_sc = weights * (grad_w - jnp.sum(weights * grad_w, axis=0, keepdims=True))
        high, low = split_bf16(grad_sc)
        k_pair = jnp.concatenate([k_high[:, :count], k_low[:, :count]], axis=0)
        q_pair = jnp.concatenate([q_high, q_low], axis=0)
        gq = dot(k_pair, high, NN)
        gq = gq[:size] + gq[size:] + dot(k_high[:, :count], low, NN)
        gk = dot(q_pair, high, NT)
        gk = gk[:size] + gk[size:] + dot(q_high, low, NT)
        gv = dot(grad_ctx, rounded, NT)
        base = pl.multiple_of(h * size, size)
        gp_s[pl.ds(base, size)] = (gq[:, :count] * scale).astype(BF)
        gp_s[pl.ds(width + base, size)] = (gk * math.log(2.0)).astype(BF)
        gp_s[pl.ds(2 * width + base, size)] = gv.astype(BF)
        return carry

    lax.fori_loop(0, HEADS, head, 0, unroll=2)

    proj_ref[...] += dot(ctx_s[...], cot_ref[...], NN)
    update_ref[...] = dot(ctx_s[...], wp_ref[...], TN).astype(BF)
    qkv_ref[...] += dot(gp_s[...], norm_s[:count], NN)
    grad_normed = dot(gp_s[...], w_ref[...], TN)
    standard, inv_scale = standardize(x_ref[...])
    grad_ref[...] = (
        inv_scale
        * (
            grad_normed
            - jnp.mean(grad_normed, axis=1, keepdims=True)
            - standard * jnp.mean(grad_normed * standard, axis=1, keepdims=True)
        )
    ).astype(BF)


def run_windows(tiles, cots, bar_q, bar_k, w_t, w_proj):
    groups, count, width = tiles.shape
    tile_spec = pl.BlockSpec((None, count, width), lambda i: (i, 0, 0))
    bar_spec = pl.BlockSpec((None, 32, LANES), lambda i: (i, 0, 0))
    whole = lambda shape: pl.BlockSpec(shape, lambda i: (0, 0))
    return pl.pallas_call(
        window_kernel,
        grid=(groups,),
        in_specs=[tile_spec, tile_spec, bar_spec, bar_spec, whole(w_t.shape), whole(w_proj.shape)],
        out_specs=[tile_spec, tile_spec, whole((3 * width, width)), whole((width, width))],
        out_shape=[
            jax.ShapeDtypeStruct(tiles.shape, BF),
            jax.ShapeDtypeStruct(tiles.shape, BF),
            jax.ShapeDtypeStruct((3 * width, width), F32),
            jax.ShapeDtypeStruct((width, width), F32),
        ],
        scratch_shapes=[
            pltpu.VMEM((LANES, width), BF),
            pltpu.VMEM((LANES, width), BF),
            pltpu.VMEM((width, LANES), F32),
            pltpu.VMEM((width, LANES), F32),
            pltpu.VMEM((width, LANES), BF),
            pltpu.VMEM((width, LANES), BF),
            pltpu.VMEM((width, count), BF),
            pltpu.VMEM((3 * width, count), BF),
        ],
        compiler_params=pltpu.CompilerParams(vmem_limit_bytes=48 * 1024 * 1024),
        cost_estimate=pl.CostEstimate(
            flops=20_000_000_000, bytes_accessed=12_000_000, transcendentals=6_000_000
        ),
    )(tiles, cots, bar_q, bar_k, w_t, w_proj)


def bar_features(labels, top, bottom):
    groups, count = labels.shape
    kinds = jnp.stack([jnp.zeros_like(top), top, bottom])
    same = (labels[:, None, :] == kinds[None, :, None]).astype(F32)
    pad = ((0, 0), (0, 29), (0, LANES - count))
    bar_q = jnp.pad(same * -BARRED, pad).astype(BF)
    bar_k = jnp.pad(1.0 - same, pad).astype(BF)
    return bar_q, bar_k


def shifted(block, axis, distance):
    devices = range(lax.axis_size(axis))
    route = [((i - distance) % len(devices), i) for i in devices]
    return lax.ppermute(block, axis, route)


def slice_levels(grid_field, starts, length, axis):

    def per_level(level_plane, offset):
        return lax.dynamic_slice_in_dim(level_plane, offset, length, axis - 1)

    return jax.vmap(per_level)(grid_field, starts)


def make_windows(grid_field):
    lev_count, grid_rows, grid_cols, model_width = grid_field.shape
    shaped = grid_field.reshape(
        lev_count, grid_rows // WLAT, WLAT, grid_cols // WLON, WLON, model_width
    )
    shaped = shaped.transpose(1, 3, 0, 2, 4, 5)
    return shaped.reshape(-1, lev_count * WLAT * WLON, model_width)


def undo_windows(blocks, lev_count, grid_rows, grid_cols):
    model_width = blocks.shape[-1]
    shaped = blocks.reshape(
        grid_rows // WLAT, grid_cols // WLON, lev_count, WLAT, WLON, model_width
    )
    return shaped.transpose(2, 0, 3, 1, 4, 5).reshape(lev_count, grid_rows, grid_cols, model_width)


def window_labels(rolled_ids, grid_cols):
    lev_count, grid_rows = rolled_ids.shape
    shaped = rolled_ids.reshape(lev_count, grid_rows // WLAT, WLAT)
    full = jnp.broadcast_to(
        shaped[:, :, :, None, None], (lev_count, grid_rows // WLAT, WLAT, grid_cols // WLON, WLON)
    )
    return full.transpose(1, 3, 0, 2, 4).reshape(-1, lev_count * WLAT * WLON)


def join_ahead_cols(grid_field, ahead_block, lon_offsets):
    lon_cols = grid_field.shape[2]
    return slice_levels(
        jnp.concatenate([grid_field, ahead_block], axis=2), lon_offsets, lon_cols, 2
    )


def join_ahead_rows(grid_field, below_rows, lat_offsets):
    lat_rows = grid_field.shape[1]
    return slice_levels(jnp.concatenate([grid_field, below_rows], axis=1), lat_offsets, lat_rows, 1)


def join_behind_rows(grid_field, above_rows, lat_offsets):
    lat_rows = grid_field.shape[1]
    return slice_levels(
        jnp.concatenate([above_rows, grid_field], axis=1), WLAT - lat_offsets, lat_rows, 1
    )


def join_behind_cols(grid_field, left_block, lon_offsets):
    lon_cols = grid_field.shape[2]
    return slice_levels(
        jnp.concatenate([left_block, grid_field], axis=2), lon_cols - lon_offsets, lon_cols, 2
    )


def local(tokens, cotangent, w_qkv, w_proj, shifts, region_ids):
    lev_count, lat_rows, lon_cols, model_width = tokens.shape
    lat_offsets = shifts[:, 0]
    lon_offsets = shifts[:, 1]
    grid_rows = lat_rows * lax.axis_size("lat")
    first_row = lax.axis_index("lat") * lat_rows
    rows_wanted = (
        first_row + lat_offsets[:, None] + jnp.arange(lat_rows, dtype=jnp.int32)[None, :]
    ) % grid_rows
    table_rows = jnp.arange(grid_rows, dtype=jnp.int32)
    rolled_ids = jnp.sum(
        jnp.where(
            rows_wanted[:, :, None] == table_rows[None, None, :], region_ids[None, None, :], 0
        ),
        axis=2,
    )
    labels = window_labels(rolled_ids, lon_cols)
    bar_q, bar_k = bar_features(labels, region_ids[0], region_ids[-1])
    ahead_tokens, ahead_cot = shifted((tokens, cotangent), "lon", -1)
    cols_tokens = join_ahead_cols(tokens, ahead_tokens, lon_offsets)
    cols_cot = join_ahead_cols(cotangent, ahead_cot, lon_offsets)
    below_tokens, below_cot = shifted((cols_tokens[:, :WLAT], cols_cot[:, :WLAT]), "lat", -1)
    rolled = join_ahead_rows(cols_tokens, below_tokens, lat_offsets)
    rolled_cot = join_ahead_rows(cols_cot, below_cot, lat_offsets)
    updates, grads_back, qkv_total, proj_total = run_windows(
        make_windows(rolled), make_windows(rolled_cot), bar_q, bar_k, w_qkv.T, w_proj
    )
    update_field = undo_windows(updates, lev_count, lat_rows, lon_cols)
    grad_field = undo_windows(grads_back, lev_count, lat_rows, lon_cols)
    above_update, above_grad = shifted(
        (update_field[:, lat_rows - WLAT :], grad_field[:, lat_rows - WLAT :]), "lat", 1
    )
    update_field = join_behind_rows(update_field, above_update, lat_offsets)
    grad_field = join_behind_rows(grad_field, above_grad, lat_offsets)
    left_update, left_grad = shifted((update_field, grad_field), "lon", 1)
    update_field = join_behind_cols(update_field, left_update, lon_offsets)
    grad_field = join_behind_cols(grad_field, left_grad, lon_offsets)
    mixed = (tokens.astype(F32) + update_field.astype(F32)).astype(BF)
    grad_tokens = (cotangent.astype(F32) + grad_field.astype(F32)).astype(BF)
    qkv_sum, proj_sum = lax.psum((qkv_total, proj_total), ("lat", "lon"))
    total_tokens = lev_count * grid_rows * lon_cols * lax.axis_size("lon")
    grad_scale = 1.0 / math.sqrt(total_tokens)
    return (mixed, grad_tokens, qkv_sum.T * grad_scale, proj_sum * grad_scale)


def solution(mesh):
    return jax.shard_map(
        local,
        mesh=mesh,
        in_specs=(P(None, "lat", "lon", None), P(None, "lat", "lon", None), P(), P(), P(), P()),
        out_specs=(P(None, "lat", "lon", None), P(None, "lat", "lon", None), P(), P()),
        check_vma=False,
    )
```

time: 570 us -> 350 us (0.61); the launches traced: 563 us -> 349 us
  matrix products: 171 us -> 0 us
  Pallas kernels: 0 us -> 75.8 us
  local copies, waits for them, and re-layouts: 99.6 us -> 51.9 us
  other arithmetic: 61.6 us -> 26.3 us
  loops' own time: 31.9 us -> 0 us
    dot_general x24 -> x0, matrix products: 171 us -> none  [the longest x2 38.4 us: window_backward(): jnp.einsum('hnm,nhe->mhe', grad_scores, queries, precision=FULL_PRECISION)]
    pallas_call x0 -> x1, Pallas kernels: none -> 75.8 us  [run_windows(): pl.pallas_call(window_kernel, grid=(groups,), in_specs=[tile_spec, tile_s...]
    sub x2 -> x0, other arithmetic: 34.4 us -> none  [window_forward(): expo = jnp.exp(scores - top_score)]
    another operation x1 -> x0, loops' own time: 31.9 us -> none  [run_groups(): return lax.scan(group_step, zero_totals, (blocks, cot_blocks, labels))]
    reshape x11 -> x2, local copies, waits for them, and re-layouts: 22.8 us -> 1.45 us  [make_windows(): return shaped.reshape(-1, lev_count * WLAT * WLON, model_width)]
    slice x10 -> x1, local copies, waits for them, and re-layouts: 11.8 us -> 1.31 us  [local(): bar_q, bar_k = bar_features(labels, region_ids[0], region_ids[-1])]
    while x96 -> x0, local copies, waits for them, and re-layouts: 7.52 us -> none
    gather x10, local copies, waits for them, and re-layouts: 26 us -> 19 us  [per_level(): return lax.dynamic_slice_in_dim(level_plane, offset, length, axis - 1)]
  transfers between devices with their start and end apart: 9 -> 9, of which waited for: 6 -> 6; matrix products, arithmetic and copies ran while one was open for 11% -> 17% of each run, Pallas kernels for 0% -> 0%
where the time goes in v1:
time: 350 us; the launch traced here: 349 us
  waiting for transfers between devices  171 us (49%)
  Pallas kernels  75.8 us (22%)
  local copies, waits for them, and re-layouts  51.9 us (15%)
  other arithmetic  26.3 us (8%)
  between operations  14.3 us (4%)
  starting transfers between devices  9.31 us (3%)
    ppermute x8, waiting for transfers between devices, shifted(): return lax.ppermute(block, axis, route)  105 us
    pallas_call x1, Pallas kernels, run_windows(): pl.pallas_call(window_kernel, grid=(groups,), in_specs=[tile_spec, tile_s...  75.8 us
    psum x1, waiting for transfers between devices, local(): qkv_sum, proj_sum = lax.psum((qkv_total, proj_total), ('lat', 'lon'))  65.8 us
    gather x10, local copies, waits for them, and re-layouts, per_level(): return lax.dynamic_slice_in_dim(level_plane, offset, length, axis - 1)  19 us
    ppermute x8, starting transfers between devices, shifted(): return lax.ppermute(block, axis, route)  9.27 us
    unnamed x20, local copies, waits for them, and re-layouts  8.46 us
  transfers between devices with their start and end apart: 9, of which 6 were waited for; matrix products, arithmetic and copies ran while one was open for 17% of the time, Pallas kernels for 0%

profile of v1, /device:TPU:0, one launch (start us, length us, event | category | flops | bytes accessed | tf_op | source)
XLA Modules:
  0.0 348.7 jit_solution(2283072982285918256)
XLA Ops:
  7.2 1.5 copy.72
  8.7 6.1 %collective-permute-start.2 = (bf16[4,24,12,512]{3,1,0,2:T(8,128)(2,1)S(1)}, bf16[4,24,12,512]{3,1,0,2:T(8,128)(2,1)}, u32[]{:S(2)}, u32[]{:S(2)}) collective-permute-start(bf16[4,24,12,512]{3,1,0,2:T(8,128)(2,1)S(1)} %copy.72), channel_id=1, source_target_pairs={{1,0},{2,1},{3,2},{4,3},{5,4},{6,5},{7,6},{0,7},{9,8},{10,9},{11,1... | collective-permute-start | bytes 3538952 | tf_op jit(solution)/shard_map/ppermute | solution.py:161
  14.8 1.1 copy.68
  15.9 0.5 collective-permute-start
  16.4 0.8 or_bitcast_fusion
  17.2 0.1 add_select_fusion
  17.3 1.5 select_reduce_fusion
  18.7 1.4 broadcast_in_dim.18
  20.1 0.7 copy.75
  20.8 0.7 broadcast_bitcast_fusion
  21.5 1.5 eq.33
  23.0 1.3 fusion.16
  24.4 2.0 pad_add_fusion
  26.3 14.8 %collective-permute-done.2 = bf16[4,24,12,512]{3,1,0,2:T(8,128)(2,1)} collective-permute-done((bf16[4,24,12,512]{3,1,0,2:T(8,128)(2,1)S(1)}, bf16[4,24,12,512]{3,1,0,2:T(8,128)(2,1)}, u32[]{:S(2)}, u32[]{:S(2)}) %collective-permute-start.2) | collective-permute-done | bytes 1179680 | tf_op jit(solution)/shard_map/ppermute | solution.py:161
  41.2 3.0 pad_maximum_fusion.1
  44.1 2.3 gather_fusion.2
  46.5 18.9 %collective-permute-done = bf16[4,24,12,512]{3,1,0,2:T(8,128)(2,1)} collective-permute-done((bf16[4,24,12,512]{3,1,0,2:T(8,128)(2,1)}, bf16[4,24,12,512]{3,1,0,2:T(8,128)(2,1)}, u32[]{:S(2)}, u32[]{:S(2)}) %collective-permute-start) | collective-permute-done | bytes 1179680 | tf_op jit(solution)/shard_map/ppermute | solution.py:161
  65.4 3.0 pad_maximum_fusion
  68.4 2.3 gather_fusion
  70.7 0.8 slice.76
  71.6 2.6 copy.76
  74.3 0.2 pad_maximum_fusion.7
  74.5 0.9 copy.73
  75.4 1.8 gather_fusion.3
  77.1 2.5 copy.74
  79.6 1.2 copy.78.cot_ref
  80.9 1.2 pad_maximum_fusion.6
  82.1 0.9 copy.69
  82.9 1.8 gather_fusion.1
  84.7 2.5 copy.70
  87.2 0.2 copy.77.x_ref
  87.5 0.8 copy-done
  88.3 75.8 %shard_map.93 = (bf16[4,288,512]{2,1,0:T(8,128)(2,1)S(1)}, bf16[4,288,512]{2,1,0:T(8,128)(2,1)S(1)}, f32[1536,512]{1,0:T(8,128)}, f32[512,512]{1,0:T(8,128)}) custom-call(bf16[4,288,512]{2,1,0:T(8,128)(2,1)S(1)} %copy.77.x_ref, bf16[4,288,512]{2,1,0:T(8,128)(2,1)} %copy.78.cot_ref, bf16[4,32,384]{2,1,0:T(8,128)(2,1)S(1)} %pad.11.bar_q_ref, ...), custom_call_target="tpu_custom_call" | custom-call | flops 20000000000 | bytes 12000000 | tf_op jit(solution)/shard_map/pallas_call | solution.py:120
  164.0 0.9 copy.79
  164.9 0.3 copy.80
  165.3 0.8 slice.78
  166.1 0.5 collective-permute-start.4
  166.5 0.9 copy.84
  167.4 0.3 copy.85
  167.8 1.2 collective-permute-start.6
  169.0 4.6 %collective-permute-done.4 = bf16[4,6,12,512]{3,2,0,1:T(8,128)(2,1)} collective-permute-done((bf16[4,6,12,512]{3,2,0,1:T(8,128)(2,1)}, bf16[4,6,12,512]{3,2,0,1:T(8,128)(2,1)}, u32[]{:S(2)}, u32[]{:S(2)}) %collective-permute-start.4) | collective-permute-done | bytes 294944 | tf_op jit(solution)/shard_map/ppermute | solution.py:161
  173.6 2.5 pad_maximum_fusion.4
  176.1 2.2 gather_fusion.4
  178.3 1.7 copy.81
  180.0 0.7 collective-permute-start.5
  180.8 2.6 pad_maximum_fusion.5
  183.3 2.2 gather_fusion.6
  185.5 0.7 copy.86
  186.2 0.2 collective-permute-start.7
  186.4 42.0 %collective-permute-done.5 = bf16[4,24,12,512]{3,1,2,0:T(8,128)(2,1)} collective-permute-done((bf16[4,24,12,512]{3,1,2,0:T(8,128)(2,1)}, bf16[4,24,12,512]{3,1,2,0:T(8,128)(2,1)}, u32[]{:S(2)}, u32[]{:S(2)}) %collective-permute-start.5) | collective-permute-done | bytes 1179680 | tf_op jit(solution)/shard_map/ppermute | solution.py:161
  228.5 1.7 copy.82
  230.2 0.8 pad_maximum_fusion.2
  231.0 2.2 copy.83
  233.2 25.0 %collective-permute-done.7 = bf16[4,24,12,512]{3,1,2,0:T(8,128)(2,1)S(1)} collective-permute-done((bf16[4,24,12,512]{3,1,2,0:T(8,128)(2,1)S(1)}, bf16[4,24,12,512]{3,1,2,0:T(8,128)(2,1)S(1)}, u32[]{:S(2)}, u32[]{:S(2)}) %collective-permute-start.7) | collective-permute-done | bytes 1179680 | tf_op jit(solution)/shard_map/ppermute | solution.py:161
  258.2 0.4 copy.87
  258.6 0.8 pad_maximum_fusion.3
  259.5 2.3 copy.88
  261.7 0.6 gather_fusion.5
  262.4 3.5 gather_fusion.7
  265.8 3.4 add_convert_fusion
  269.2 65.8 %all-reduce.7.cloned.1.call-done = (f32[1536,512]{1,0:T(8,128)}, f32[512,512]{1,0:T(8,128)}) async-done(((f32[1536,512]{1,0:T(8,128)}, f32[512,512]{1,0:T(8,128)}), (f32[1536,512]{1,0:T(8,128)}, f32[512,512]{1,0:T(8,128)})) %all-reduce.7.cloned.1.call-update) | async-done | bytes 4194320 | tf_op jit(solution)/shard_map/psum | solution.py:263
  334.9 2.3 multiply_bitcast_fusion
  337.2 2.4 copy.89
  339.6 2.3 broadcast_multiply_fusion
  (27 shorter events, 0.4 us)
Async XLA Ops:
  7.2 7.6 %copy-start.1 = (bf16[4,24,12,512]{3,1,2,0:T(8,128)(2,1)S(1)}, bf16[4,24,12,512]{3,1,2,0:T(8,128)(2,1)}, u32[]{:S(2)}) copy-start(bf16[4,24,12,512]{3,1,2,0:T(8,128)(2,1)} %param.6) | copy-start | bytes 3538948
  7.2 327.8 %all-reduce.7.cloned.1.call-start = ((), (), s32[]{:S(2)}) async-start(), calls=%async_computation | async-start | bytes 8388608 | tf_op jit(solution)/shard_map/psum | solution.py:263
  8.7 32.4 %copy-start.3 = (bf16[4,24,12,512]{3,1,2,0:T(8,128)(2,1)S(1)}, bf16[4,24,12,512]{3,1,2,0:T(8,128)(2,1)}, u32[]{:S(2)}) copy-start(bf16[4,24,12,512]{3,1,2,0:T(8,128)(2,1)} %param.7) | copy-start | bytes 3538948
  8.7 32.4 %collective-permute-start.2 = (bf16[4,24,12,512]{3,1,0,2:T(8,128)(2,1)S(1)}, bf16[4,24,12,512]{3,1,0,2:T(8,128)(2,1)}, u32[]{:S(2)}, u32[]{:S(2)}) collective-permute-start(bf16[4,24,12,512]{3,1,0,2:T(8,128)(2,1)S(1)} %copy.72), channel_id=1, source_target_pairs={{1,0},{2,1},{3,2},{4,3},{5,4},{6,5},{7,6},{0,7},{9,8},{10,9},{11,1... | collective-permute-start | bytes 3538952 | tf_op jit(solution)/shard_map/ppermute | solution.py:161
  15.9 49.5 %collective-permute-start = (bf16[4,24,12,512]{3,1,0,2:T(8,128)(2,1)}, bf16[4,24,12,512]{3,1,0,2:T(8,128)(2,1)}, u32[]{:S(2)}, u32[]{:S(2)}) collective-permute-start(bf16[4,24,12,512]{3,1,0,2:T(8,128)(2,1)} %copy.68), channel_id=1, source_target_pairs={{1,0},{2,1},{3,2},{4,3},{5,4},{6,5},{7,6},{0,7},{9,8},{10,9},{11,1... | collective-permute-start | bytes 3538952 | tf_op jit(solution)/shard_map/ppermute | solution.py:161
  46.5 27.8 %collective-permute-start.3 = (bf16[4,6,12,512]{3,1,2,0:T(8,128)(2,1)S(1)}, bf16[4,6,12,512]{3,1,2,0:T(8,128)(2,1)S(1)}, u32[]{:S(2)}, u32[]{:S(2)}) collective-permute-start(bf16[4,6,12,512]{3,1,2,0:T(8,128)(2,1)S(1)} %slice.77), channel_id=1, source_target_pairs={{8,0},{16,8},{24,16},{0,24},{9,1},{17,9},{25,17},{1,25},{10,2},{18... | collective-permute-start | bytes 884744 | tf_op jit(solution)/shard_map/ppermute | solution.py:161
  68.4 3.2 copy-start.6
  68.4 3.2 copy-start.7
  71.4 9.4 %collective-permute-start.1 = (bf16[4,6,12,512]{3,1,2,0:T(8,128)(2,1)}, bf16[4,6,12,512]{3,1,2,0:T(8,128)(2,1)}, u32[]{:S(2)}, u32[]{:S(2)}) collective-permute-start(bf16[4,6,12,512]{3,1,2,0:T(8,128)(2,1)} %slice.76), channel_id=1, source_target_pairs={{8,0},{16,8},{24,16},{0,24},{9,1},{17,9},{25,17},{1,25},{10,2},{18... | collective-permute-start | bytes 884744 | tf_op jit(solution)/shard_map/ppermute | solution.py:161
  87.2 1.0 copy-start
  166.1 7.5 %collective-permute-start.4 = (bf16[4,6,12,512]{3,2,0,1:T(8,128)(2,1)}, bf16[4,6,12,512]{3,2,0,1:T(8,128)(2,1)}, u32[]{:S(2)}, u32[]{:S(2)}) collective-permute-start(bf16[4,6,12,512]{3,2,0,1:T(8,128)(2,1)} %slice.78), channel_id=1, source_target_pairs={{24,0},{0,8},{8,16},{16,24},{25,1},{1,9},{9,17},{17,25},{26,2},{2,... | collective-permute-start | bytes 884744 | tf_op jit(solution)/shard_map/ppermute | solution.py:161
  167.8 13.0 %collective-permute-start.6 = (bf16[4,6,12,512]{3,2,0,1:T(8,128)(2,1)S(1)}, bf16[4,6,12,512]{3,2,0,1:T(8,128)(2,1)}, u32[]{:S(2)}, u32[]{:S(2)}) collective-permute-start(bf16[4,6,12,512]{3,2,0,1:T(8,128)(2,1)S(1)} %slice.79), channel_id=1, source_target_pairs={{24,0},{0,8},{8,16},{16,24},{25,1},{1,9},{9,17},{17,25},{26,2},{2,... | collective-permute-start | bytes 884744 | tf_op jit(solution)/shard_map/ppermute | solution.py:161
  180.0 48.5 %collective-permute-start.5 = (bf16[4,24,12,512]{3,1,2,0:T(8,128)(2,1)}, bf16[4,24,12,512]{3,1,2,0:T(8,128)(2,1)}, u32[]{:S(2)}, u32[]{:S(2)}) collective-permute-start(bf16[4,24,12,512]{3,1,2,0:T(8,128)(2,1)} %copy.81), channel_id=1, source_target_pairs={{7,0},{0,1},{1,2},{2,3},{3,4},{4,5},{5,6},{6,7},{15,8},{8,9},{9,10... | collective-permute-start | bytes 3538952 | tf_op jit(solution)/shard_map/ppermute | solution.py:161
  186.2 72.0 %collective-permute-start.7 = (bf16[4,24,12,512]{3,1,2,0:T(8,128)(2,1)S(1)}, bf16[4,24,12,512]{3,1,2,0:T(8,128)(2,1)S(1)}, u32[]{:S(2)}, u32[]{:S(2)}) collective-permute-start(bf16[4,24,12,512]{3,1,2,0:T(8,128)(2,1)S(1)} %copy.86), channel_id=1, source_target_pairs={{7,0},{0,1},{1,2},{2,3},{3,4},{4,5},{5,6},{6,7},{15,8},{8,9},{9,10... | collective-permute-start | bytes 3538952 | tf_op jit(solution)/shard_map/ppermute | solution.py:161
  259.4 2.3 copy-start.5
  262.3 3.5 copy-start.2
  262.4 3.5 copy-start.4
Sparse Core Ops, SparseCore 0:
  169.1 165.8 all-reduce.6
